TPU v7x, 512 devices: a whole 4x4x16 slice. The times are simulated.
512 devices in a mesh: segment: 8 (over y, core), vocab: 64 (over z, x).
Axes of the slice: x: 4, y: 4, z: 16, core: 2. Of those that a mesh axis runs over, the one named last changes fastest.
Arguments:
- hidden: bfloat16 [16384, 8192], P('vocab', 'segment'), may hold values from -160 to 160
- norm_gain: float32 [8192], P('segment'), may hold values from 0.5 to 1.5
- head: bfloat16 [65536, 8192], P('vocab', 'segment'), may hold values from -3 to 3
- allowed: int32 [4, 16384], P(None, 'vocab'), may hold values from 0 to 127, as said below
- target_slot: int32 [16384], P('vocab'), may hold values from 0 to 3
- target_offset: int32 [16384], P('vocab'), may hold values from 0 to 511
Outputs:
- logprob: float32 [16384], P('vocab')
Inputs may be any that keep to these rules, and one draw needn't show every extreme that they name: `allowed`: the 4 blocks of a token are distinct. Among the 256 tokens of one index of vocab, a block is named by at most 16 of them; in every draw some block is named by exactly 16 tokens of every index of vocab.
All inputs are finite; a program needn't handle non-finite values.
Results may differ from a plain program's by a relative error of at most 0.00083.
Values may be sent and summed in bfloat16 or wider, within the bound.
A program may use at most 64 MiB of HBM per device.

v0:
```python
import jax
import jax.numpy as jnp
from jax import lax
from jax.sharding import PartitionSpec as P

D = 8192
BLOCK = 512
A = 4


def block_stats(logits, targets):
    peak_value = jnp.max(logits, axis=-1)
    exp_total = jnp.sum(jnp.exp(logits - peak_value[..., None]), axis=-1)
    column = lax.broadcasted_iota(jnp.int32, logits.shape, logits.ndim - 1)
    target_logit = jnp.sum(
        jnp.where(column == targets[..., None], logits, jnp.zeros_like(logits)), axis=-1
    )
    return (peak_value, exp_total, target_logit)


def per_device(hidden, norm_gain, head, allowed, target_slot, target_offset):
    tok_count = hidden.shape[0]
    slab_width = hidden.shape[1]
    vocab_size = lax.axis_size("vocab")
    blk_dev = head.shape[0] // BLOCK
    blk_count = blk_dev * vocab_size
    capacity = 2 * tok_count * A // blk_count
    widened = hidden.astype(jnp.float32)
    squares = lax.psum(jnp.sum(widened * widened, axis=1), "segment")
    normed = (widened * lax.rsqrt(squares / D + 1e-05)[:, None] * norm_gain[None, :]).astype(
        jnp.bfloat16
    )
    entries = allowed.reshape(-1)
    onehot = (entries[:, None] == jnp.arange(blk_count, dtype=jnp.int32)[None, :]).astype(jnp.int32)
    before = jnp.cumsum(onehot, axis=0) - onehot
    position = jnp.sum(before * onehot, axis=1)
    slot_index = entries * capacity + position
    slot_total = blk_count * capacity
    entry_token = jnp.tile(jnp.arange(tok_count, dtype=jnp.int32), A)
    slot_token = jnp.full((slot_total,), tok_count, jnp.int32).at[slot_index].set(entry_token)
    entry_choice = jnp.repeat(jnp.arange(A, dtype=jnp.int32), tok_count)
    entry_target = jnp.where(
        entry_choice == jnp.tile(target_slot, A), jnp.tile(target_offset, A), -1
    )
    slot_target = jnp.full((slot_total,), -1, jnp.int32).at[slot_index].set(entry_target)
    padded = jnp.concatenate([normed, jnp.zeros((1, slab_width), jnp.bfloat16)], axis=0)
    outgoing = padded[slot_token].reshape(vocab_size, blk_dev, capacity, slab_width)
    incoming, wanted = (
        lax.all_to_all(outgoing, "vocab", split_axis=0, concat_axis=0, tiled=True),
        lax.all_to_all(
            slot_target.reshape(vocab_size, blk_dev, capacity),
            "vocab",
            split_axis=0,
            concat_axis=0,
            tiled=True,
        ),
    )
    weights = head.reshape(blk_dev, BLOCK, slab_width)
    logits = lax.psum(
        jnp.einsum("sbcd,bvd->sbcv", incoming, weights, preferred_element_type=jnp.float32),
        "segment",
    )
    peak_value, exp_total, target_logit = block_stats(logits, wanted)
    peak_value, exp_total, target_logit = (
        lax.all_to_all(peak_value, "vocab", split_axis=0, concat_axis=0, tiled=True),
        lax.all_to_all(exp_total, "vocab", split_axis=0, concat_axis=0, tiled=True),
        lax.all_to_all(target_logit, "vocab", split_axis=0, concat_axis=0, tiled=True),
    )
    peak_value = peak_value.reshape(-1)[slot_index].reshape(A, tok_count)
    exp_total = exp_total.reshape(-1)[slot_index].reshape(A, tok_count)
    target_logit = target_logit.reshape(-1)[slot_index].reshape(A, tok_count)
    largest = jnp.max(peak_value, axis=0)
    log_total = largest + jnp.log(
        jnp.sum(exp_total * jnp.exp(peak_value - largest[None, :]), axis=0)
    )
    return jnp.sum(target_logit, axis=0) - log_total


def solution(mesh):
    return jax.shard_map(
        per_device,
        mesh=mesh,
        in_specs=(
            P("vocab", "segment"),
            P("segment"),
            P("vocab", "segment"),
            P(None, "vocab"),
            P("vocab"),
            P("vocab"),
        ),
        out_specs=P("vocab"),
        check_vma=False,
    )
```

profile of v0, /device:TPU:2, one launch (start us, length us, event | category | flops | bytes accessed | tf_op | source)
XLA Modules:
  0.0 419.9 jit_solution(16631843202107226767)
XLA Ops:
  6.5 0.0 copy-start
  6.5 0.0 copy-start.1
  6.5 0.0 all-reduce.3.cloned.1.call-start
  6.5 0.8 eq.41
  7.4 0.7 multiply_bitcast_fusion
  8.1 0.1 copy.27
  8.2 0.2 fusion.10
  8.5 0.1 copy.28
  8.6 0.7 copy.36
  9.3 0.4 fusion.9
  9.7 4.3 %scatter_custom_fusion.1 = s32[2048]{0:T(1024)S(1)} fusion(s32[1024]{0:T(1024)S(1)} %bitcast.39, s32[1024]{0:T(1024)S(1)} %bitcast.43, s32[]{:T(128)} %constant.7.clone.1), kind=kCustom, calls=%fused_computation.32 | custom fusion | bytes 8196 | tf_op jit(solution)/shard_map/scatter | solution.py:40
  14.0 1.2 fusion.5
  15.2 14.9 %psum.14 = f32[256]{0:T(256)S(1)} all-reduce(f32[256]{0:T(256)S(1)} %fusion.5), channel_id=1, replica_groups=mesh['segment'=8,'vocab'=64] {'segment'}, use_global_device_ids=true, to_apply=%region_5.6 | all-reduce | flops 256 | bytes 2048 | tf_op jit(solution)/shard_map/psum | solution.py:29
  30.1 0.0 copy-done.1
  30.1 0.9 fusion.7
  31.0 9.7 %gather_fusion = bf16[2048,1024]{1,0:T(8,128)(2,1)} fusion(bf16[257,1024]{1,0:T(8,128)(2,1)S(1)} %concatenate.3, s32[2048]{0:T(1024)S(1)} %fusion.13), kind=kCustom, calls=%fused_computation | custom fusion | bytes 8396800 | tf_op jit(solution)/shard_map/gather | solution.py:47
  40.7 206.4 %all_to_all.25 = bf16[64,2,16,1024]{3,2,1,0:T(8,128)(2,1)S(1)} all-to-all(bf16[64,2,16,1024]{3,2,1,0:T(8,128)(2,1)} %bitcast.35), channel_id=1, replica_groups=mesh['segment'=8,'vocab'=64] {'vocab'}, dimensions={0} | all-to-all | bytes 8388608 | tf_op jit(solution)/shard_map/all_to_all | solution.py:49
  247.1 0.0 copy-done
  247.1 4.3 %fusion.2 = f32[64,2,16,512]{3,2,0,1:T(8,128)} fusion(bf16[2,512,1024,1]{2,1,3,0:T(8,128)(2,1)S(1)} %bitcast.34, bf16[64,2,16,1024]{3,2,1,0:T(8,128)(2,1)S(1)} %all_to_all.25), kind=kOutput, calls=%fused_computation.11 | convolution fusion | flops 2147483648 | bytes 10485760 | tf_op jit(solution)/shard_map/sbcd,bvd->sbcv/dot_general | solution.py:60
  251.5 0.0 copy-start.2
  251.5 0.0 copy-start.3
  251.5 0.0 all-reduce.3.cloned.1.call-update
  251.5 0.7 copy-done.2
  252.1 0.0 copy-done.3
  252.2 4.3 %scatter_custom_fusion = s32[2048]{0:T(1024)S(1)} fusion(s32[1024]{0:T(1024)S(1)} %bitcast.40, s32[1024]{0:T(1024)S(1)} %bitcast.44, s32[]{:T(128)} %constant.11.clone.1), kind=kCustom, calls=%fused_computation.37 | custom fusion | bytes 8196 | tf_op jit(solution)/shard_map/scatter | solution.py:45
  256.5 0.1 reshape.85
  256.6 19.9 %all_to_all.26 = s32[64,2,16]{2,1,0:T(2,128)S(1)} all-to-all(s32[64,2,16]{2,1,0:T(2,128)S(1)} %reshape.85), channel_id=1, replica_groups=mesh['segment'=8,'vocab'=64] {'vocab'}, dimensions={0} | all-to-all | bytes 16384 | tf_op jit(solution)/shard_map/all_to_all | solution.py:50
  276.5 53.9 %all-reduce.3.cloned.1.call-done = f32[64,2,16,512]{3,2,0,1:T(8,128)} async-done(((f32[64,2,16,512]{3,2,0,1:T(8,128)}), f32[64,2,16,512]{3,2,0,1:T(8,128)}) %all-reduce.3.cloned.1.call-update) | async-done | bytes 4194320 | tf_op jit(solution)/shard_map/psum | solution.py:59
  330.4 2.5 reduce_max.18
  332.9 3.2 exponential_reduce_fusion
  336.1 0.7 copy.33
  336.7 15.7 %all-to-all-start.4 = ((f32[64,2,16]{2,1,0:T(2,128)}), f32[64,2,16]{2,1,0:T(2,128)S(1)}, u32[]{:S(2)}, u32[]{:S(2)}) async-start(f32[64,2,16]{2,1,0:T(2,128)} %copy.33), calls=%async_computation.4 | async-start | bytes 131072 | tf_op jit(solution)/shard_map/all_to_all | solution.py:66
  352.4 0.7 copy.32
  353.1 13.5 %all-to-all-done.4 = f32[64,2,16]{2,1,0:T(2,128)S(1)} async-done(((f32[64,2,16]{2,1,0:T(2,128)}), f32[64,2,16]{2,1,0:T(2,128)S(1)}, u32[]{:S(2)}, u32[]{:S(2)}) %all-to-all-start.4) | async-done | bytes 8224 | tf_op jit(solution)/shard_map/all_to_all | solution.py:66
  366.6 5.6 %all-to-all-start.3 = ((f32[64,2,16]{2,1,0:T(2,128)}), f32[64,2,16]{2,1,0:T(2,128)S(1)}, u32[]{:S(2)}, u32[]{:S(2)}) async-start(f32[64,2,16]{2,1,0:T(2,128)} %copy.32), calls=%async_computation.3 | async-start | bytes 131072 | tf_op jit(solution)/shard_map/all_to_all | solution.py:65
  372.2 0.7 copy.31
  372.9 13.6 %all-to-all-done.3 = f32[64,2,16]{2,1,0:T(2,128)S(1)} async-done(((f32[64,2,16]{2,1,0:T(2,128)}), f32[64,2,16]{2,1,0:T(2,128)S(1)}, u32[]{:S(2)}, u32[]{:S(2)}) %all-to-all-start.3) | async-done | bytes 8224 | tf_op jit(solution)/shard_map/all_to_all | solution.py:65
  386.4 5.5 %all-to-all-start.2 = ((f32[64,2,16]{2,1,0:T(2,128)}), f32[64,2,16]{2,1,0:T(2,128)S(1)}, u32[]{:S(2)}, u32[]{:S(2)}) async-start(f32[64,2,16]{2,1,0:T(2,128)} %copy.31), calls=%async_computation.2 | async-start | bytes 131072 | tf_op jit(solution)/shard_map/all_to_all | solution.py:67
  392.0 0.1 reshape.92
  392.1 6.2 %gather_fusion.3 = f32[1024]{0:T(1024)S(1)} fusion(f32[2048]{0:T(1024)S(1)} %reshape.92, s32[1024]{0:T(1024)S(1)} %broadcast_clamp_fusion), kind=kCustom, calls=%fused_computation.3 | custom fusion | bytes 12288 | tf_op jit(solution)/shard_map/gather | solution.py:70
  398.3 0.1 reshape.90
  398.4 6.2 %gather_fusion.2 = f32[1024]{0:T(1024)S(1)} fusion(f32[2048]{0:T(1024)S(1)} %reshape.90, s32[1024]{0:T(1024)S(1)} %broadcast_clamp_fusion), kind=kCustom, calls=%fused_computation.2 | custom fusion | bytes 12288 | tf_op jit(solution)/shard_map/gather | solution.py:69
  404.6 1.5 all-to-all-done.2
  406.1 0.1 reshape.88
  406.2 6.2 %gather_fusion.1 = f32[1024]{0:T(1024)S(1)} fusion(f32[2048]{0:T(1024)S(1)} %reshape.88, s32[1024]{0:T(1024)S(1)} %broadcast_clamp_fusion), kind=kCustom, calls=%fused_computation.1 | custom fusion | bytes 12288 | tf_op jit(solution)/shard_map/gather | solution.py:71
  412.5 0.6 add_subtract_fusion
  (21 shorter events, 0.3 us)
Async XLA Ops:
  6.5 240.6 %copy-start = (bf16[1024,1024]{1,0:T(8,128)(2,1)S(1)}, bf16[1024,1024]{1,0:T(8,128)(2,1)}, u32[]{:S(2)}) copy-start(bf16[1024,1024]{1,0:T(8,128)(2,1)} %param.8) | copy-start | bytes 6291460
  6.5 23.6 %copy-start.1 = (bf16[256,1024]{1,0:T(8,128)(2,1)S(1)}, bf16[256,1024]{1,0:T(8,128)(2,1)}, u32[]{:S(2)}) copy-start(bf16[256,1024]{1,0:T(8,128)(2,1)} %param.6) | copy-start | bytes 1572868
  6.5 323.8 %all-reduce.3.cloned.1.call-start = ((), (), s32[]{:S(2)}) async-start(), calls=%async_computation.5 | async-start | bytes 8388608 | tf_op jit(solution)/shard_map/psum | solution.py:59
  251.5 0.7 copy-start.2
  251.5 0.7 copy-start.3
  336.7 29.9 %all-to-all-start.4 = ((f32[64,2,16]{2,1,0:T(2,128)}), f32[64,2,16]{2,1,0:T(2,128)S(1)}, u32[]{:S(2)}, u32[]{:S(2)}) async-start(f32[64,2,16]{2,1,0:T(2,128)} %copy.33), calls=%async_computation.4 | async-start | bytes 131072 | tf_op jit(solution)/shard_map/all_to_all | solution.py:66
  366.6 19.8 %all-to-all-start.3 = ((f32[64,2,16]{2,1,0:T(2,128)}), f32[64,2,16]{2,1,0:T(2,128)S(1)}, u32[]{:S(2)}, u32[]{:S(2)}) async-start(f32[64,2,16]{2,1,0:T(2,128)} %copy.32), calls=%async_computation.3 | async-start | bytes 131072 | tf_op jit(solution)/shard_map/all_to_all | solution.py:65
  386.4 19.7 %all-to-all-start.2 = ((f32[64,2,16]{2,1,0:T(2,128)}), f32[64,2,16]{2,1,0:T(2,128)S(1)}, u32[]{:S(2)}, u32[]{:S(2)}) async-start(f32[64,2,16]{2,1,0:T(2,128)} %copy.31), calls=%async_computation.2 | async-start | bytes 131072 | tf_op jit(solution)/shard_map/all_to_all | solution.py:67
Sparse Core Ops, SparseCore 0:
  251.6 78.7 all-reduce.2
where the time goes:
time: 420 us
  blocking collectives  241 us (57%)
  waiting for transfers between devices  82.5 us (20%)
  local copies, waits for them, and re-layouts  41.8 us (10%)
  starting transfers between devices  26.8 us (6%)
  between operations  13.6 us (3%)
  other arithmetic  9.78 us (2%)
  matrix products  4.34 us (1%)
    all_to_all x1, blocking collectives, per_device(): lax.all_to_all(outgoing, 'vocab', split_axis=0, concat_axis=0, tiled=True)  206 us
    psum x1, waiting for transfers between devices, per_device(): lax.psum(jnp.einsum('sbcd,bvd->sbcv', incoming, weights, preferred_elemen...  53.9 us
    all_to_all x1, blocking collectives, per_device(): lax.all_to_all(slot_target.reshape(vocab_size, blk_dev, capacity), 'vocab...  19.9 us
    all_to_all x1, starting transfers between devices, per_device(): lax.all_to_all(exp_total, 'vocab', split_axis=0, concat_axis=0, tiled=True)  15.7 us
    psum x1, blocking collectives, per_device(): squares = lax.psum(jnp.sum(widened * widened, axis=1), 'segment')  14.9 us
    all_to_all x1, waiting for transfers between devices, per_device(): lax.all_to_all(peak_value, 'vocab', split_axis=0, concat_axis=0, tiled=True)  13.6 us
    all_to_all x1, waiting for transfers between devices, per_device(): lax.all_to_all(exp_total, 'vocab', split_axis=0, concat_axis=0, tiled=True)  13.5 us
    gather x1, local copies, waits for them, and re-layouts, per_device(): padded[slot_token].reshape(vocab_size, blk_dev, capacity, slab_width)  9.67 us
  transfers between devices with their start and end apart: 4, of which 4 were waited for; matrix products, arithmetic and copies ran while one was open for 4% of the time, Pallas kernels for 0%

commit v1 on v0

--- a/solution.py
+++ b/solution.py
@@ -56,9 +56,12 @@
         ),
     )
     weights = head.reshape(blk_dev, BLOCK, slab_width)
-    logits = lax.psum(
-        jnp.einsum("sbcd,bvd->sbcv", incoming, weights, preferred_element_type=jnp.float32),
-        "segment",
+    logits = jnp.sum(
+        lax.all_gather(
+            jnp.einsum("sbcd,bvd->sbcv", incoming, weights, preferred_element_type=jnp.float32),
+            "segment",
+        ),
+        axis=0,
     )
     peak_value, exp_total, target_logit = block_stats(logits, wanted)
     peak_value, exp_total, target_logit = (

time: 420 us -> 513 us (1.22)
  the two profiles are of different devices: /device:TPU:2 before, /device:TPU:8 now
where the time goes in v1:
time: 513 us; the launch traced here: 512 us
  blocking collectives  240 us (47%)
  waiting for transfers between devices  163 us (32%)
  local copies, waits for them, and re-layouts  41.8 us (8%)
  starting transfers between devices  25 us (5%)
  other arithmetic  24.9 us (5%)
  between operations  13.6 us (3%)
    all_to_all x1, blocking collectives, per_device(): lax.all_to_all(outgoing, 'vocab', split_axis=0, concat_axis=0, tiled=True)  204 us
    all_gather x1, waiting for transfers between devices, per_device(): lax.all_gather(jnp.einsum('sbcd,bvd->sbcv', incoming, weights, preferred_...  131 us
    all_to_all x1, blocking collectives, per_device(): lax.all_to_all(slot_target.reshape(vocab_size, blk_dev, capacity), 'vocab...  20.9 us
    all_to_all x1, starting transfers between devices, per_device(): lax.all_to_all(exp_total, 'vocab', split_axis=0, concat_axis=0, tiled=True)  15.6 us
    reduce_sum x1, other arithmetic, per_device(): jnp.sum(lax.all_gather(jnp.einsum('sbcd,bvd->sbcv', incoming, weights, pr...  15.1 us
    all_to_all x1, waiting for transfers between devices, per_device(): lax.all_to_all(exp_total, 'vocab', split_axis=0, concat_axis=0, tiled=True)  14.8 us
    psum x1, blocking collectives, per_device(): squares = lax.psum(jnp.sum(widened * widened, axis=1), 'segment')  14.8 us
    all_to_all x1, waiting for transfers between devices, per_device(): lax.all_to_all(peak_value, 'vocab', split_axis=0, concat_axis=0, tiled=True)  14.6 us
  transfers between devices with their start and end apart: 4, of which 4 were waited for; matrix products, arithmetic and copies ran while one was open for 4% of the time, Pallas kernels for 0%

profile of v1, /device:TPU:8, one launch (start us, length us, event | category | flops | bytes accessed | tf_op | source)
XLA Modules:
  0.0 512.0 jit_solution(9575952722907549198)
XLA Ops:
  6.5 0.0 copy-start
  6.5 0.0 copy-start.1
  6.5 0.0 all-gather.3.cloned.1.call-start
  6.5 0.8 eq.41
  7.4 0.7 multiply_bitcast_fusion
  8.1 0.1 copy.30
  8.2 0.2 fusion.10
  8.5 0.1 copy.31
  8.6 0.7 copy.39
  9.3 0.4 fusion.9
  9.7 4.3 scatter_custom_fusion.1
  14.0 1.2 fusion.5
  15.2 14.8 %psum.7 = f32[256]{0:T(256)S(1)} all-reduce(f32[256]{0:T(256)S(1)} %fusion.5), channel_id=1, replica_groups=mesh['segment'=8,'vocab'=64] {'segment'}, use_global_device_ids=true, to_apply=%region_5.6 | all-reduce | flops 256 | bytes 2048 | tf_op jit(solution)/shard_map/psum | solution.py:29
  30.0 0.0 copy-done.1
  30.0 0.9 fusion.7
  30.9 9.7 %gather_fusion = bf16[2048,1024]{1,0:T(8,128)(2,1)} fusion(bf16[257,1024]{1,0:T(8,128)(2,1)S(1)} %concatenate.3, s32[2048]{0:T(1024)S(1)} %fusion.13), kind=kCustom, calls=%fused_computation | custom fusion | bytes 8396800 | tf_op jit(solution)/shard_map/gather | solution.py:47
  40.6 203.9 %all_to_all.25 = bf16[64,2,16,1024]{3,2,1,0:T(8,128)(2,1)S(1)} all-to-all(bf16[64,2,16,1024]{3,2,1,0:T(8,128)(2,1)} %bitcast.37), channel_id=1, replica_groups=mesh['segment'=8,'vocab'=64] {'vocab'}, dimensions={0} | all-to-all | bytes 8388608 | tf_op jit(solution)/shard_map/all_to_all | solution.py:49
  244.6 0.0 copy-done
  244.6 4.4 fusion.2
  249.0 0.0 copy-start.2
  249.0 0.0 copy-start.3
  249.0 0.0 all-gather.3.cloned.1.call-update
  249.0 0.7 copy-done.2
  249.7 0.0 copy-done.3
  249.7 4.3 scatter_custom_fusion
  254.0 0.1 reshape.85
  254.1 20.9 %all_to_all.26 = s32[64,2,16]{2,1,0:T(2,128)S(1)} all-to-all(s32[64,2,16]{2,1,0:T(2,128)S(1)} %reshape.85), channel_id=1, replica_groups=mesh['segment'=8,'vocab'=64] {'vocab'}, dimensions={0} | all-to-all | bytes 16384 | tf_op jit(solution)/shard_map/all_to_all | solution.py:50
  275.0 130.8 %all-gather.3.cloned.1.call-done = f32[512,2,16,512]{3,2,0,1:T(8,128)} async-done(((f32[64,2,16,512]{3,2,0,1:T(8,128)}), f32[512,2,16,512]{3,2,0,1:T(8,128)}) %all-gather.3.cloned.1.call-update) | async-done | bytes 33554448 | tf_op jit(solution)/shard_map/all_gather | solution.py:60
  405.8 15.1 %reduce_sum.68 = f32[64,2,16,512]{3,2,0,1:T(8,128)} reduce(f32[8,64,2,16,512]{4,3,1,0,2:T(8,128)} %bitcast.36, f32[]{:T(128)} %constant.15.clone.1), dimensions={0}, to_apply=%region_7.8 | reduce | flops 7340032 | bytes 37748740 | tf_op jit(solution)/shard_map/reduce_sum | solution.py:59
  421.0 2.5 reduce_max.18
  423.5 3.2 exponential_reduce_fusion
  426.7 0.7 copy.36
  427.4 15.6 %all-to-all-start.4 = ((f32[64,2,16]{2,1,0:T(2,128)}), f32[64,2,16]{2,1,0:T(2,128)S(1)}, u32[]{:S(2)}, u32[]{:S(2)}) async-start(f32[64,2,16]{2,1,0:T(2,128)} %copy.36), calls=%async_computation.4 | async-start | bytes 131072 | tf_op jit(solution)/shard_map/all_to_all | solution.py:69
  443.0 0.7 copy.35
  443.6 14.8 %all-to-all-done.4 = f32[64,2,16]{2,1,0:T(2,128)S(1)} async-done(((f32[64,2,16]{2,1,0:T(2,128)}), f32[64,2,16]{2,1,0:T(2,128)S(1)}, u32[]{:S(2)}, u32[]{:S(2)}) %all-to-all-start.4) | async-done | bytes 8224 | tf_op jit(solution)/shard_map/all_to_all | solution.py:69
  458.4 4.8 all-to-all-start.3
  463.2 0.7 copy.34
  463.9 14.6 %all-to-all-done.3 = f32[64,2,16]{2,1,0:T(2,128)S(1)} async-done(((f32[64,2,16]{2,1,0:T(2,128)}), f32[64,2,16]{2,1,0:T(2,128)S(1)}, u32[]{:S(2)}, u32[]{:S(2)}) %all-to-all-start.3) | async-done | bytes 8224 | tf_op jit(solution)/shard_map/all_to_all | solution.py:68
  478.5 4.6 all-to-all-start.2
  483.1 0.1 reshape.92
  483.2 6.2 %gather_fusion.3 = f32[1024]{0:T(1024)S(1)} fusion(f32[2048]{0:T(1024)S(1)} %reshape.92, s32[1024]{0:T(1024)S(1)} %broadcast_clamp_fusion), kind=kCustom, calls=%fused_computation.3 | custom fusion | bytes 12288 | tf_op jit(solution)/shard_map/gather | solution.py:73
  489.4 0.1 reshape.90
  489.5 6.2 %gather_fusion.2 = f32[1024]{0:T(1024)S(1)} fusion(f32[2048]{0:T(1024)S(1)} %reshape.90, s32[1024]{0:T(1024)S(1)} %broadcast_clamp_fusion), kind=kCustom, calls=%fused_computation.2 | custom fusion | bytes 12288 | tf_op jit(solution)/shard_map/gather | solution.py:72
  495.7 2.6 all-to-all-done.2
  498.3 0.1 reshape.88
  498.4 6.2 %gather_fusion.1 = f32[1024]{0:T(1024)S(1)} fusion(f32[2048]{0:T(1024)S(1)} %reshape.88, s32[1024]{0:T(1024)S(1)} %broadcast_clamp_fusion), kind=kCustom, calls=%fused_computation.1 | custom fusion | bytes 12288 | tf_op jit(solution)/shard_map/gather | solution.py:74
  504.6 0.6 add_subtract_fusion
  (21 shorter events, 0.3 us)
Async XLA Ops:
  6.5 238.0 %copy-start = (bf16[1024,1024]{1,0:T(8,128)(2,1)S(1)}, bf16[1024,1024]{1,0:T(8,128)(2,1)}, u32[]{:S(2)}) copy-start(bf16[1024,1024]{1,0:T(8,128)(2,1)} %param.8) | copy-start | bytes 6291460
  6.5 23.5 %copy-start.1 = (bf16[256,1024]{1,0:T(8,128)(2,1)S(1)}, bf16[256,1024]{1,0:T(8,128)(2,1)}, u32[]{:S(2)}) copy-start(bf16[256,1024]{1,0:T(8,128)(2,1)} %param.6) | copy-start | bytes 1572868
  6.5 399.3 %all-gather.3.cloned.1.call-start = ((), (), s32[]{:S(2)}) async-start(), calls=%async_computation.5 | async-start | bytes 37748736 | tf_op jit(solution)/shard_map/all_gather | solution.py:60
  249.0 0.7 copy-start.2
  249.0 0.7 copy-start.3
  427.4 31.1 %all-to-all-start.4 = ((f32[64,2,16]{2,1,0:T(2,128)}), f32[64,2,16]{2,1,0:T(2,128)S(1)}, u32[]{:S(2)}, u32[]{:S(2)}) async-start(f32[64,2,16]{2,1,0:T(2,128)} %copy.36), calls=%async_computation.4 | async-start | bytes 131072 | tf_op jit(solution)/shard_map/all_to_all | solution.py:69
  458.4 20.1 %all-to-all-start.3 = ((f32[64,2,16]{2,1,0:T(2,128)}), f32[64,2,16]{2,1,0:T(2,128)S(1)}, u32[]{:S(2)}, u32[]{:S(2)}) async-start(f32[64,2,16]{2,1,0:T(2,128)} %copy.35), calls=%async_computation.3 | async-start | bytes 131072 | tf_op jit(solution)/shard_map/all_to_all | solution.py:68
  478.5 19.8 %all-to-all-start.2 = ((f32[64,2,16]{2,1,0:T(2,128)}), f32[64,2,16]{2,1,0:T(2,128)S(1)}, u32[]{:S(2)}, u32[]{:S(2)}) async-start(f32[64,2,16]{2,1,0:T(2,128)} %copy.34), calls=%async_computation.2 | async-start | bytes 131072 | tf_op jit(solution)/shard_map/all_to_all | solution.py:70
Sparse Core Ops, SparseCore 0:
  249.1 156.6 all-gather.2
